TPU v7x, 512 devices: a whole 4x4x16 slice. The times are simulated.
512 devices in a mesh: block: 64 (over z, y_lo, core), day: 8 (over x, y_hi).
Axes of the slice: x: 4, y: 4 (y_hi: 2, y_lo: 2; y = y_hi * 2 + y_lo), z: 16, core: 2. Of those that a mesh axis runs over, the one named last changes fastest.
Arguments:
- traces: float32 [8, 4096, 2400], P('day', 'block'), may hold values from -6 to 6
- counts: int32 [64], replicated, may hold values from 1 to 64, 3072 in all
- order: int32 [64], replicated, may hold values from 0 to 63, each once
Outputs:
- stacks: float32 [3, 64, 61, 4096], P(None, 'day', None, 'block')
Inputs may be any that keep to these rules, and one draw needn't show every extreme that they name: Slots from counts[b] to 63 of block b hold no channel; some block holds exactly 64. `order`: a permutation of the blocks; the window takes its first 3 entries as owners.
All inputs are finite; a program needn't handle non-finite values.
Results may differ from a plain program's by a relative error of at most 0.0037.
Values may be sent and summed in bfloat16 or wider, within the bound.
A program may use at most 128 MiB of HBM per device.

v0:
```python
import jax
import jax.numpy as jnp
from jax import lax
from jax.sharding import PartitionSpec as P

SEG = 2400
LAGS = 61
STEPS = 3
HALF = 30
clip_level = 2.5


def broadcast(value, axis, source):
    kept = jnp.where(lax.axis_index(axis) == source, value, 0).astype(value.dtype)
    return lax.psum(kept, axis)


def every_lag(padded, own_three):
    seg_len = own_three.shape[2]
    sums = []
    for lag in range(LAGS):
        window = padded[:, :, lag : lag + seg_len]
        sums.append(
            jnp.einsum("jsu,csu->jc", window, own_three, preferred_element_type=jnp.float32)
        )
    return jnp.stack(sums, 1)


def lag_sums(own_rows, owner_rows):
    capacity, samples = own_rows.shape
    owner_count = owner_rows.shape[0]
    segments = samples // SEG
    padded = jnp.pad(owner_rows.reshape(owner_count, segments, SEG), ((0, 0), (0, 0), (HALF, HALF)))
    own_three = own_rows.reshape(capacity, segments, SEG)
    return every_lag(padded, own_three)


def per_device(traces, counts, order):
    capacity = traces.shape[1]
    samples = traces.shape[2]
    block_index = lax.axis_index("block")
    live_count = lax.dynamic_index_in_dim(counts, block_index, 0, keepdims=False)
    pieces = traces[0].reshape(capacity, samples // SEG, SEG)
    centered = pieces - jnp.mean(pieces, axis=2, keepdims=True)
    rms = jnp.sqrt(jnp.mean(centered * centered, axis=2, keepdims=True) + 1e-05)
    slot = jnp.arange(capacity, dtype=jnp.int32)
    live = (slot < live_count).astype(jnp.float32)
    white = jnp.clip(centered / rms, -clip_level, clip_level) * live[:, None, None]
    own_rows = white.astype(jnp.bfloat16).reshape(capacity, samples)
    day_count = lax.axis_size("day")
    scale = float(day_count * samples) ** (-0.5)
    results = []
    for step in range(STEPS):
        owner_rows = broadcast(own_rows, "block", order[step])
        partial_value = lag_sums(own_rows, owner_rows)
        results.append(lax.psum_scatter(partial_value, "day", scatter_dimension=0, tiled=True))
    stacked = jnp.stack(results, 0)
    return stacked * scale


def solution(mesh):
    in_specs = (P("day", "block", None), P(), P())
    out_specs = P(None, "day", None, "block")
    return jax.shard_map(
        per_device, mesh=mesh, in_specs=in_specs, out_specs=out_specs, check_vma=False
    )
```

profile of v0, /device:TPU:32, one launch (start us, length us, event | category | flops | bytes accessed | tf_op | source)
XLA Modules:
  0.0 758.6 jit_solution(11040752436789546314)
XLA Ops:
  6.5 1.2 dynamic_slice.4
  8.4 1.2 reduce_sum.18
  9.7 1.4 fusion.187
  11.1 1.4 fusion.914
  14.4 2.0 broadcast_select_fusion.2
  17.6 433.5 %all-reduce.6.cloned.1.call-done = (bf16[64,2400]{1,0:T(8,128)(2,1)}, bf16[64,2400]{1,0:T(8,128)(2,1)}, bf16[64,2400]{1,0:T(8,128)(2,1)}) async-done(((bf16[64,2400]{1,0:T(8,128)(2,1)}, bf16[64,2400]{1,0:T(8,128)(2,1)}, bf16[64,2400]{1,0:T(8,128)(2,1)}), (bf16[64,2400]{1,0:T(8,128)(2,1)}, bf16[64,2400]{1,0:T(8,128)(2,1)}, bf16[64,2400]{1,0:T(8,128)(2,1)})) %all-reduce.6.cloned.1.call-update) | async-done | bytes 921616 | tf_op jit(solution)/shard_map/psum | solution.py:15
  451.1 1.3 fusion.121
  452.4 1.3 fusion.120
  453.7 1.3 fusion.119
  472.4 1.3 copy-done.4
  492.4 1.2 fusion.182
  493.6 0.9 fusion.181
  494.5 0.9 fusion.180
  495.4 0.9 fusion.179
  496.3 0.9 fusion.178
  497.2 0.9 fusion.177
  498.1 1.1 fusion.176
  499.2 0.9 fusion.175
  500.1 0.9 fusion.174
  501.0 0.9 fusion.173
  501.9 0.9 fusion.172
  503.7 0.9 fusion.170
  504.6 0.9 fusion.169
  505.5 0.9 fusion.168
  506.4 0.9 fusion.167
  507.3 0.9 fusion.166
  508.2 0.9 fusion.165
  509.1 0.9 fusion.164
  510.0 0.9 fusion.163
  510.9 0.9 fusion.162
  512.7 0.9 fusion.160
  514.5 0.9 fusion.158
  515.4 0.9 fusion.157
  516.3 0.9 fusion.156
  518.1 0.9 fusion.154
  520.7 0.9 fusion.151
  521.6 0.9 fusion.150
  523.4 0.9 fusion.148
  524.3 0.9 fusion.147
  525.2 0.9 fusion.146
  527.0 0.9 fusion.144
  529.7 0.9 fusion.141
  530.6 0.9 fusion.140
  531.5 0.9 fusion.139
  532.4 0.9 fusion.138
  533.4 0.9 fusion.137
  534.2 0.9 fusion.136
  535.2 0.9 fusion.135
  536.1 0.9 fusion.134
  537.0 0.9 fusion.133
  537.9 0.9 fusion.132
  538.8 0.9 fusion.131
  539.7 0.9 fusion.130
  540.7 0.9 fusion.129
  541.6 0.9 fusion.128
  542.5 0.9 fusion.127
  543.4 0.9 fusion.126
  544.3 0.9 fusion.125
  546.1 0.9 fusion.123
  547.0 0.9 fusion.122
  547.9 16.5 %reduce-scatter.6.cloned.1.call-done = f32[8,61,64]{2,0,1:T(8,128)} async-done(((f32[64,61,64]{2,0,1:T(8,128)}), f32[8,61,64]{2,0,1:T(8,128)}) %reduce-scatter.6.cloned.1.call-update) | async-done | bytes 124944 | tf_op jit(solution)/shard_map/reduce_scatter | solution.py:56
  564.4 92.8 %reduce-scatter.8.cloned.1.call-done = f32[8,61,64]{2,0,1:T(8,128)} async-done(((f32[64,61,64]{2,0,1:T(8,128)}), f32[8,61,64]{2,0,1:T(8,128)}) %reduce-scatter.8.cloned.1.call-update) | async-done | bytes 124944 | tf_op jit(solution)/shard_map/reduce_scatter | solution.py:56
  657.2 92.8 %reduce-scatter.4.cloned.1.call-done = f32[8,61,64]{2,0,1:T(8,128)} async-done(((f32[64,61,64]{2,0,1:T(8,128)}), f32[8,61,64]{2,0,1:T(8,128)}) %reduce-scatter.4.cloned.1.call-update) | async-done | bytes 124944 | tf_op jit(solution)/shard_map/reduce_scatter | solution.py:56
  750.0 2.1 maximum_multiply_fusion
  (154 shorter events, 46.9 us)
Async XLA Ops:
  6.5 444.5 %all-reduce.6.cloned.1.call-start = ((), (), s32[]{:S(2)}) async-start(), calls=%async_computation.6 | async-start | bytes 1867776 | tf_op jit(solution)/shard_map/psum | solution.py:15
  9.6 7.7 %copy-start.3 = (f32[1,64,2400]{2,1,0:T(8,128)S(1)}, f32[1,64,2400]{2,1,0:T(8,128)}, u32[]{:S(2)}) copy-start(f32[1,64,2400]{2,1,0:T(8,128)} %param.3) | copy-start | bytes 1843204
  17.3 547.1 %reduce-scatter.6.cloned.1.call-start = ((), (), s32[]{:S(2)}) async-start(), calls=%async_computation.4 | async-start | bytes 2248704 | tf_op jit(solution)/shard_map/reduce_scatter | solution.py:56
  451.1 3.9 copy-start.2
  471.5 2.5 copy-start.1
  472.4 1.3 copy-start.4
  473.8 183.4 %reduce-scatter.8.cloned.1.call-start = ((), (), s32[]{:S(2)}) async-start(), calls=%async_computation.5 | async-start | bytes 2248704 | tf_op jit(solution)/shard_map/reduce_scatter | solution.py:56
  490.6 1.8 copy-start
  492.4 6.8 copy-start.5
  539.7 210.3 %reduce-scatter.4.cloned.1.call-start = ((), (), s32[]{:S(2)}) async-start(), calls=%async_computation.3 | async-start | bytes 2248704 | tf_op jit(solution)/shard_map/reduce_scatter | solution.py:56
Sparse Core Ops, SparseCore 0:
  17.4 433.5 all-reduce.5
  473.9 90.4 reduce-scatter.5
  569.8 87.3 reduce-scatter.7
  662.4 87.4 reduce-scatter.3
where the time goes:
time: 759 us
  waiting for transfers between devices  636 us (84%)
  matrix products  94.2 us (12%)
  between operations  16 us (2%)
  other arithmetic  8.43 us (1%)
    psum x1, waiting for transfers between devices, broadcast(): return lax.psum(kept, axis)  434 us
    reduce_scatter x3, waiting for transfers between devices, per_device(): lax.psum_scatter(partial_value, 'day', scatter_dimension=0, tiled=True)  202 us
    dot_general x183, matrix products, every_lag(): jnp.einsum('jsu,csu->jc', window, own_three, preferred_element_type=jnp.f...  94.2 us
  transfers between devices with their start and end apart: 4, of which 4 were waited for; matrix products, arithmetic and copies ran while one was open for 10% of the time, Pallas kernels for 0%

commit v1 on v0

--- a/solution.py
+++ b/solution.py
@@ -12,7 +12,7 @@
 
 def broadcast(value, axis, source):
     kept = jnp.where(lax.axis_index(axis) == source, value, 0).astype(value.dtype)
-    return lax.psum(kept, axis)
+    return jnp.sum(lax.all_gather(kept, axis), axis=0)
 
 
 def every_lag(padded, own_three):

time: 759 us -> 731 us (0.963)
  waiting for transfers between devices: 636 us -> 578 us
  other arithmetic: 8.43 us -> 40.3 us
    psum x1 -> x0, waiting for transfers between devices: 434 us -> none  [broadcast(): return lax.psum(kept, axis)]
    all_gather x0 -> x3, waiting for transfers between devices: none -> 334 us  [broadcast(): return jnp.sum(lax.all_gather(kept, axis), axis=0)]
    reduce_scatter x3, waiting for transfers between devices: 202 us -> 243 us  [per_device(): lax.psum_scatter(partial_value, 'day', scatter_dimension=0, tiled=True)]
    reduce_sum x0 -> x3, other arithmetic: none -> 31.8 us  [broadcast(): return jnp.sum(lax.all_gather(kept, axis), axis=0)]
  transfers between devices with their start and end apart: 4 -> 6, of which waited for: 4 -> 6; matrix products, arithmetic and copies ran while one was open for 10% -> 17% of each run, Pallas kernels for 0% -> 0%
where the time goes in v1:
time: 731 us
  waiting for transfers between devices  578 us (79%)
  matrix products  91.5 us (13%)
  other arithmetic  40.3 us (6%)
  between operations  16.4 us (2%)
    all_gather x3, waiting for transfers between devices, broadcast(): return jnp.sum(lax.all_gather(kept, axis), axis=0)  334 us
    reduce_scatter x3, waiting for transfers between devices, per_device(): lax.psum_scatter(partial_value, 'day', scatter_dimension=0, tiled=True)  243 us
    dot_general x183, matrix products, every_lag(): jnp.einsum('jsu,csu->jc', window, own_three, preferred_element_type=jnp.f...  91.5 us
    reduce_sum x3, other arithmetic, broadcast(): return jnp.sum(lax.all_gather(kept, axis), axis=0)  31.8 us
  transfers between devices with their start and end apart: 6, of which 6 were waited for; matrix products, arithmetic and copies ran while one was open for 17% of the time, Pallas kernels for 0%

profile of v1, /device:TPU:32, one launch (start us, length us, event | category | flops | bytes accessed | tf_op | source)
XLA Modules:
  0.0 730.7 jit_solution(7907347389886921547)
XLA Ops:
  6.5 1.2 dynamic_slice.4
  8.4 1.2 reduce_sum.54
  9.7 1.4 fusion.190
  11.1 1.4 fusion.916
  14.4 2.0 broadcast_select_fusion.2
  16.4 0.9 broadcast_select_fusion.1
  19.1 144.7 %all-gather.6.cloned.1.call-done = bf16[64,64,2400]{2,1,0:T(8,128)(2,1)} async-done(((bf16[1,64,2400]{2,1,0:T(8,128)(2,1)}), bf16[64,64,2400]{2,1,0:T(8,128)(2,1)}) %all-gather.6.cloned.1.call-update) | async-done | bytes 19660816 | tf_op jit(solution)/shard_map/all_gather | solution.py:15
  163.7 10.5 %reduce_sum.57 = bf16[64,2400]{1,0:T(8,128)(2,1)S(1)} reduce(bf16[64,64,2400]{2,1,0:T(8,128)(2,1)} %all-gather.6.cloned.1.call-done, bf16[]{:T(256)} %constant.30.clone.1), dimensions={0}, to_apply=%region_4.5 | reduce | flops 9676800 | bytes 19968002 | tf_op jit(solution)/shard_map/reduce_sum | solution.py:15
  174.3 131.2 %all-gather.8.cloned.1.call-done = bf16[64,64,2400]{2,1,0:T(8,128)(2,1)} async-done(((bf16[1,64,2400]{2,1,0:T(8,128)(2,1)}), bf16[64,64,2400]{2,1,0:T(8,128)(2,1)}) %all-gather.8.cloned.1.call-update) | async-done | bytes 19660816 | tf_op jit(solution)/shard_map/all_gather | solution.py:15
  305.5 10.5 %reduce_sum.58 = bf16[64,2400]{1,0:T(8,128)(2,1)S(1)} reduce(bf16[64,64,2400]{2,1,0:T(8,128)(2,1)} %all-gather.8.cloned.1.call-done, bf16[]{:T(256)} %constant.30.clone.1), dimensions={0}, to_apply=%region_6.7 | reduce | flops 9676800 | bytes 19968002 | tf_op jit(solution)/shard_map/reduce_sum | solution.py:15
  334.6 1.2 fusion.121
  335.7 0.9 fusion.120
  336.6 0.9 fusion.119
  338.4 0.9 fusion.117
  339.3 0.9 fusion.116
  340.2 1.1 fusion.115
  341.3 0.9 fusion.114
  342.2 0.9 fusion.113
  343.1 0.9 fusion.112
  344.0 0.9 fusion.111
  344.9 0.9 fusion.110
  345.8 0.9 fusion.109
  346.7 0.9 fusion.108
  348.5 0.9 fusion.106
  349.4 0.9 fusion.105
  350.3 0.9 fusion.104
  351.2 0.9 fusion.103
  352.1 0.9 fusion.102
  353.1 0.9 fusion.101
  355.7 0.9 fusion.98
  356.7 0.9 fusion.97
  357.6 0.9 fusion.96
  359.4 0.9 fusion.94
  361.2 0.9 fusion.92
  362.1 0.9 fusion.91
  363.0 0.9 fusion.90
  363.9 0.9 fusion.89
  364.8 0.9 fusion.88
  366.6 0.9 fusion.86
  367.5 0.9 fusion.85
  369.3 0.9 fusion.83
  370.2 0.9 fusion.82
  372.0 0.9 fusion.80
  373.8 0.9 fusion.78
  374.7 0.9 fusion.77
  375.6 0.9 fusion.76
  376.5 0.9 fusion.75
  377.4 0.9 fusion.74
  379.2 0.9 fusion.72
  380.1 0.9 fusion.71
  381.0 0.9 fusion.70
  382.8 0.9 fusion.68
  383.7 0.9 fusion.67
  384.6 0.9 fusion.66
  385.5 0.9 fusion.65
  386.4 0.9 fusion.64
  388.2 0.9 fusion.62
  390.1 57.6 %all-gather.4.cloned.1.call-done = bf16[64,64,2400]{2,1,0:T(8,128)(2,1)} async-done(((bf16[1,64,2400]{2,1,0:T(8,128)(2,1)}), bf16[64,64,2400]{2,1,0:T(8,128)(2,1)}) %all-gather.4.cloned.1.call-update) | async-done | bytes 19660816 | tf_op jit(solution)/shard_map/all_gather | solution.py:15
  447.7 10.8 %reduce_sum.56 = bf16[64,2400]{1,0:T(8,128)(2,1)S(1)} reduce(bf16[64,64,2400]{2,1,0:T(8,128)(2,1)} %all-gather.4.cloned.1.call-done, bf16[]{:T(256)} %constant.30.clone.1), dimensions={0}, to_apply=%region_2.3 | reduce | flops 9676800 | bytes 19968002 | tf_op jit(solution)/shard_map/reduce_sum | solution.py:15
  477.0 1.3 copy-done.2
  478.3 59.3 %reduce-scatter.8.cloned.1.call-done = f32[8,61,64]{2,0,1:T(8,128)} async-done(((f32[64,61,64]{2,0,1:T(8,128)}), f32[8,61,64]{2,0,1:T(8,128)}) %reduce-scatter.8.cloned.1.call-update) | async-done | bytes 124944 | tf_op jit(solution)/shard_map/reduce_scatter | solution.py:56
  537.6 92.1 %reduce-scatter.6.cloned.1.call-done = f32[8,61,64]{2,0,1:T(8,128)} async-done(((f32[64,61,64]{2,0,1:T(8,128)}), f32[8,61,64]{2,0,1:T(8,128)}) %reduce-scatter.6.cloned.1.call-update) | async-done | bytes 124944 | tf_op jit(solution)/shard_map/reduce_scatter | solution.py:56
  629.7 92.0 %reduce-scatter.4.cloned.1.call-done = f32[8,61,64]{2,0,1:T(8,128)} async-done(((f32[64,61,64]{2,0,1:T(8,128)}), f32[8,61,64]{2,0,1:T(8,128)}) %reduce-scatter.4.cloned.1.call-update) | async-done | bytes 124944 | tf_op jit(solution)/shard_map/reduce_scatter | solution.py:56
  721.7 2.1 maximum_multiply_fusion
  (175 shorter events, 51.1 us)
Async XLA Ops:
  6.5 157.2 %all-gather.6.cloned.1.call-start = ((), (), s32[]{:S(2)}) async-start(), calls=%async_computation.5 | async-start | bytes 20234240 | tf_op jit(solution)/shard_map/all_gather | solution.py:15
  8.4 10.4 %copy-start.6 = (f32[64]{0:T(128)}, f32[64]{0:T(128)S(1)}, u32[]{:S(2)}) copy-start(f32[64]{0:T(128)S(1)} %compare_convert_fusion) | copy-start | bytes 772
  9.7 9.2 %copy-start = (f32[1,64,2400]{2,1,0:T(8,128)S(1)}, f32[1,64,2400]{2,1,0:T(8,128)}, u32[]{:S(2)}) copy-start(f32[1,64,2400]{2,1,0:T(8,128)} %param.3) | copy-start | bytes 1843204
  9.7 9.4 %copy-start.3 = (f32[64]{0:T(128)}, f32[64]{0:T(128)S(1)}, u32[]{:S(2)}) copy-start(f32[64]{0:T(128)S(1)} %broadcast_multiply_fusion) | copy-start | bytes 772
  11.1 8.0 %copy-start.9 = (f32[64]{0:T(128)}, f32[64]{0:T(128)S(1)}, u32[]{:S(2)}) copy-start(f32[64]{0:T(128)S(1)} %add_sqrt_fusion) | copy-start | bytes 772
  17.3 288.2 %all-gather.8.cloned.1.call-start = ((), (), s32[]{:S(2)}) async-start(), calls=%async_computation.7 | async-start | bytes 20234240 | tf_op jit(solution)/shard_map/all_gather | solution.py:15
  18.1 429.7 %all-gather.4.cloned.1.call-start = ((), (), s32[]{:S(2)}) async-start(), calls=%async_computation.3 | async-start | bytes 20234240 | tf_op jit(solution)/shard_map/all_gather | solution.py:15
  18.8 518.8 %reduce-scatter.8.cloned.1.call-start = ((), (), s32[]{:S(2)}) async-start(), calls=%async_computation.8 | async-start | bytes 2248704 | tf_op jit(solution)/shard_map/reduce_scatter | solution.py:56
  323.3 1.8 copy-start.4
  323.3 1.8 copy-start.7
  323.3 1.8 copy-start.10
  334.5 6.8 copy-start.1
  356.7 5.4 copy-start.5
  356.7 5.4 copy-start.8
  356.7 5.4 copy-start.11
  390.0 239.6 %reduce-scatter.6.cloned.1.call-start = ((), (), s32[]{:S(2)}) async-start(), calls=%async_computation.6 | async-start | bytes 2248704 | tf_op jit(solution)/shard_map/reduce_scatter | solution.py:56
  474.2 247.5 %reduce-scatter.4.cloned.1.call-start = ((), (), s32[]{:S(2)}) async-start(), calls=%async_computation.4 | async-start | bytes 2248704 | tf_op jit(solution)/shard_map/reduce_scatter | solution.py:56
  477.0 1.3 copy-start.2
Sparse Core Ops, SparseCore 0:
  17.4 146.2 all-gather.5
  165.9 139.5 all-gather.7
  307.7 140.0 all-gather.3
  452.3 85.2 reduce-scatter.7
  542.1 87.5 reduce-scatter.5
  634.2 87.4 reduce-scatter.3
